TPU v7x, 32 devices: a whole 2x2x4 slice. The times are simulated.
32 devices in a mesh: groups: 2 (over y), row: 8 (over z, x), col: 2 (over core).
Axes of the slice: x: 2, y: 2, z: 4, core: 2. Of those that a mesh axis runs over, the one named last changes fastest.
Arguments:
- tokens: bfloat16 [2048, 4096], P(('groups', 'row'), 'col'), parts along dimension 0, may hold values from -6 to 6
- cotangent: bfloat16 [2048, 4096], P(('groups', 'row'), 'col'), parts along dimension 0, may hold values from -0.5 to 0.5
- gate_weight: bfloat16 [14336, 4096], P('row', 'col'), may hold values from -0.09375 to 0.09375
- up_weight: bfloat16 [14336, 4096], P('row', 'col'), may hold values from -0.09375 to 0.09375
- down_weight: bfloat16 [14336, 4096], P('row', 'col'), may hold values from -0.046875 to 0.046875
- gate_dir: bfloat16 [14336, 4096], P('row', 'col'), may hold values from -0.09375 to 0.09375
- up_dir: bfloat16 [14336, 4096], P('row', 'col'), may hold values from -0.09375 to 0.09375
- down_dir: bfloat16 [14336, 4096], P('row', 'col'), may hold values from -0.046875 to 0.046875
Outputs:
- hvp_gate: bfloat16 [28672, 4096], P(('groups', 'row'), 'col'), parts along dimension 0
- hvp_up: bfloat16 [28672, 4096], P(('groups', 'row'), 'col'), parts along dimension 0
- hvp_down: bfloat16 [28672, 4096], P(('groups', 'row'), 'col'), parts along dimension 0
There are 2 independent parts, one for each index of `groups`. A program takes and returns all parts, laid end to end along the dimension named above; an argument that names none is the same for every part. Nothing has to cross between parts.
All inputs are finite; a program needn't handle non-finite values.
Results may differ from a plain program's by a relative error of at most 0.0051.
Values may be sent and summed in bfloat16 or wider, within the bound.
No kernel may reach another device: no remote copies, remote signals or barrier semaphores. Data moves between devices by JAX's collectives and lax.ppermute only.
A program may use at most 320 MiB of HBM per device.

v0:
```python
import jax
import jax.numpy as jnp
from jax import lax
from jax.sharding import PartitionSpec as P


def second_order(forward_sum, backward_sum, hidden_count):
    gate_value = forward_sum[:hidden_count]
    up_value = forward_sum[hidden_count : 2 * hidden_count]
    gate_tangent = forward_sum[2 * hidden_count : 3 * hidden_count]
    up_tangent = forward_sum[3 * hidden_count :]
    grad_hidden = backward_sum[:hidden_count]
    grad_tangent = backward_sum[hidden_count:]
    sigmoid_gate = jax.nn.sigmoid(gate_value)
    activation = gate_value * sigmoid_gate
    first_slope = sigmoid_gate * (1.0 + gate_value * (1.0 - sigmoid_gate))
    second_slope = (
        sigmoid_gate * (1.0 - sigmoid_gate) * (2.0 + gate_value * (1.0 - 2.0 * sigmoid_gate))
    )
    hidden_dot = first_slope * gate_tangent * up_value + activation * up_tangent
    gate_dot = (
        grad_tangent * up_value + grad_hidden * up_tangent
    ) * first_slope + grad_hidden * up_value * second_slope * gate_tangent
    up_dot = grad_tangent * activation + grad_hidden * first_slope * gate_tangent
    return jnp.concatenate((gate_dot, up_dot, hidden_dot), axis=0).astype(jnp.bfloat16)


def shards(tokens, cotangent, gate_weight, up_weight, down_weight, gate_dir, up_dir, down_dir):
    hidden_count = gate_weight.shape[0]
    forward_stack = jnp.concatenate((gate_weight, up_weight, gate_dir, up_dir), axis=0)
    backward_stack = jnp.concatenate((down_weight, down_dir), axis=0)
    contract = (((1,), (1,)), ((), ()))
    token_rows = lax.all_gather(tokens, "row", axis=0, tiled=True)
    cot_rows = lax.all_gather(cotangent, "row", axis=0, tiled=True)
    forward_terms = lax.dot_general(
        forward_stack, token_rows, contract, preferred_element_type=jnp.float32
    )
    backward_terms = lax.dot_general(
        backward_stack, cot_rows, contract, preferred_element_type=jnp.float32
    )
    forward_sum, backward_sum = lax.psum((forward_terms, backward_terms), "col")
    results = second_order(forward_sum, backward_sum, hidden_count)
    paired_terms = results[: 2 * hidden_count]
    hidden_terms = results[2 * hidden_count :]
    paired = jnp.dot(paired_terms, token_rows, preferred_element_type=jnp.float32)
    down_total = jnp.dot(hidden_terms, cot_rows, preferred_element_type=jnp.float32)
    hvp_gate = paired[:hidden_count].astype(jnp.bfloat16)
    hvp_up = paired[hidden_count:].astype(jnp.bfloat16)
    hvp_down = down_total.astype(jnp.bfloat16)
    return (hvp_gate, hvp_up, hvp_down)


def solution(mesh):
    in_specs = (
        P(("groups", "row"), "col"),
        P(("groups", "row"), "col"),
        P("row", "col"),
        P("row", "col"),
        P("row", "col"),
        P("row", "col"),
        P("row", "col"),
        P("row", "col"),
    )
    out_specs = (
        P(("groups", "row"), "col"),
        P(("groups", "row"), "col"),
        P(("groups", "row"), "col"),
    )
    return jax.shard_map(shards, mesh=mesh, in_specs=in_specs, out_specs=out_specs, check_vma=False)
```

profile of v0, /device:TPU:13, one launch (start us, length us, event | category | flops | bytes accessed | tf_op | source)
XLA Modules:
  0.0 416.1 jit_solution(2009889012345145043)
XLA Ops:
  7.2 0.0 all-gather.3.cloned.1.call-start
  7.2 0.7 all-gather.3.cloned.1.call-update
  7.9 0.0 all-gather.5.cloned.1.call-start
  7.9 0.7 all-gather.5.cloned.1.call-update
  8.6 0.0 all-reduce.3.cloned.1.call-start
  8.7 74.3 %all-gather.3.cloned.1.call-done = bf16[1024,2048]{1,0:T(8,128)(2,1)} async-done(((bf16[128,2048]{1,0:T(8,128)(2,1)}), bf16[1024,2048]{1,0:T(8,128)(2,1)}) %all-gather.3.cloned.1.call-update) | async-done | bytes 4194320 | tf_op jit(solution)/shard_map/all_gather | solution.py:34
  83.0 22.0 %fusion.8 = f32[3584,1024]{1,0:T(8,128)} fusion(bf16[1024,2048]{1,0:T(8,128)(2,1)} %all-gather.3.cloned.1.call-done, bf16[1792,2048]{1,0:T(8,128)(2,1)} %param.15, bf16[1792,2048]{1,0:T(8,128)(2,1)} %param.12), kind=kOutput, calls=%fused_computation.9 | convolution fusion | flops 15061745664 | bytes 33554432 | tf_op jit(solution)/shard_map/dot_general | solution.py:38
  104.9 51.9 %all-gather.5.cloned.1.call-done = bf16[1024,2048]{1,0:T(8,128)(2,1)} async-done(((bf16[128,2048]{1,0:T(8,128)(2,1)}), bf16[1024,2048]{1,0:T(8,128)(2,1)}) %all-gather.5.cloned.1.call-update) | async-done | bytes 4194320 | tf_op jit(solution)/shard_map/all_gather | solution.py:33
  156.8 50.4 %fusion = f32[7168,1024]{1,0:T(8,128)} fusion(bf16[1024,2048]{1,0:T(8,128)(2,1)} %all-gather.5.cloned.1.call-done, bf16[1792,2048]{1,0:T(8,128)(2,1)} %param.14, bf16[1792,2048]{1,0:T(8,128)(2,1)} %param.13, bf16[1792,2048]{1,0:T(8,128)(2,1)} %param.11, bf16[1792,2048]{1,0:T(8,128)(2,1)} %param.10), kind=kOutput, calls=%fused_computation | convolution fusion | flops 30182211584 | bytes 62914560 | tf_op jit(solution)/shard_map/dot_general | solution.py:35
  207.2 0.0 all-reduce.3.cloned.1.call-update
  207.3 130.9 %all-reduce.3.cloned.1.call-done = (f32[3584,1024]{1,0:T(8,128)}, f32[7168,1024]{1,0:T(8,128)}) async-done(((f32[3584,1024]{1,0:T(8,128)}, f32[7168,1024]{1,0:T(8,128)}), (f32[3584,1024]{1,0:T(8,128)}, f32[7168,1024]{1,0:T(8,128)})) %all-reduce.3.cloned.1.call-update) | async-done | bytes 44040208 | tf_op jit(solution)/shard_map/psum | solution.py:41
  338.2 19.4 %fusion.18 = (bf16[1792,1024]{1,0:T(8,128)(2,1)}, bf16[1792,1024]{1,0:T(8,128)(2,1)}) fusion(f32[7168,1024]{1,0:T(8,128)} %get-tuple-element.4, f32[3584,1024]{1,0:T(8,128)} %get-tuple-element.3), kind=kLoop, calls=%fused_computation.22 | loop fusion | flops 51380224 | bytes 51380224 | tf_op jit(solution)/shard_map/convert.2
  357.5 22.4 %convolution_convert_fusion = bf16[3584,2048]{1,0:T(8,128)(2,1)} fusion(bf16[1024,2048]{1,0:T(8,128)(2,1)} %all-gather.5.cloned.1.call-done, bf16[1792,1024]{1,0:T(8,128)(2,1)} %get-tuple-element.6, bf16[1792,1024]{1,0:T(8,128)(2,1)} %get-tuple-element.5), kind=kOutput, calls=%fused_computation.8 | convolution fusion | flops 15054405632 | bytes 26214400 | tf_op jit(solution)/shard_map/dot_general | solution.py:45
  380.0 0.0 copy-start
  380.0 11.1 %fusion.29 = (bf16[1792,2048]{1,0:T(8,128)(2,1)}, bf16[1792,2048]{1,0:T(8,128)(2,1)}) fusion(bf16[3584,2048]{1,0:T(8,128)(2,1)} %convolution_convert_fusion), kind=kLoop, calls=%fused_computation.34 | loop fusion | bytes 29360128 | tf_op jit(solution)/shard_map/slice | solution.py:48
  391.0 0.0 copy-done
  391.0 18.5 %convolution_convert_fusion.1 = bf16[1792,2048]{1,0:T(8,128)(2,1)} fusion(bf16[1024,2048]{1,0:T(8,128)(2,1)S(1)} %copy-done, f32[7168,1024]{1,0:T(8,128)} %get-tuple-element.4), kind=kOutput, calls=%fused_computation.15 | convolution fusion | flops 7543717888 | bytes 40894464 | tf_op jit(solution)/shard_map/dot_general | solution.py:46
Async XLA Ops:
  7.2 75.8 %all-gather.3.cloned.1.call-start = ((), (), s32[]{:S(2)}) async-start(), calls=%async_computation | async-start | bytes 4718592 | tf_op jit(solution)/shard_map/all_gather | solution.py:34
  7.9 148.9 %all-gather.5.cloned.1.call-start = ((), (), s32[]{:S(2)}) async-start(), calls=%async_computation.1 | async-start | bytes 4718592 | tf_op jit(solution)/shard_map/all_gather | solution.py:33
  8.6 329.5 %all-reduce.3.cloned.1.call-start = ((), (), s32[]{:S(2)}) async-start(), calls=%async_computation.2 | async-start | bytes 88080384 | tf_op jit(solution)/shard_map/psum | solution.py:41
  380.0 11.1 %copy-start = (bf16[1024,2048]{1,0:T(8,128)(2,1)S(1)}, bf16[1024,2048]{1,0:T(8,128)(2,1)}, u32[]{:S(2)}) copy-start(bf16[1024,2048]{1,0:T(8,128)(2,1)} %all-gather.3.cloned.1.call-done) | copy-start | bytes 12582916
Sparse Core Ops, SparseCore 0:
  10.1 72.8 all-gather.2
  85.1 71.6 all-gather.4
  207.4 130.7 all-reduce.2
where the time goes:
time: 417 us; the launch traced here: 416 us
  waiting for transfers between devices  258 us (62%)
  matrix products  113 us (27%)
  other arithmetic  19.4 us (5%)
  between operations  13.7 us (3%)
  local copies, waits for them, and re-layouts  11.1 us (3%)
    psum x1, waiting for transfers between devices, shards(): forward_sum, backward_sum = lax.psum((forward_terms, backward_terms), 'col')  131 us
    all_gather x1, waiting for transfers between devices, shards(): cot_rows = lax.all_gather(cotangent, 'row', axis=0, tiled=True)  74.3 us
    all_gather x1, waiting for transfers between devices, shards(): token_rows = lax.all_gather(tokens, 'row', axis=0, tiled=True)  51.9 us
    dot_general x1, matrix products, shards(): lax.dot_general(forward_stack, token_rows, contract, preferred_element_ty...  50.4 us
    dot_general x1, matrix products, shards(): jnp.dot(paired_terms, token_rows, preferred_element_type=jnp.float32)  22.4 us
    dot_general x1, matrix products, shards(): lax.dot_general(backward_stack, cot_rows, contract, preferred_element_typ...  22 us
    another operation x1, other arithmetic  19.4 us
    dot_general x1, matrix products, shards(): jnp.dot(hidden_terms, cot_rows, preferred_element_type=jnp.float32)  18.5 us
  transfers between devices with their start and end apart: 3, of which 3 were waited for; matrix products, arithmetic and copies ran while one was open for 5% of the time, Pallas kernels for 0%

commit v1 on v0

v1 whole, which is shorter than its diff:
```python
import jax
import jax.numpy as jnp
from jax import lax
from jax.experimental import pallas as pl
from jax.experimental.pallas import tpu as pltpu
from jax.sharding import PartitionSpec as P

F32 = jnp.float32
BF16 = jnp.bfloat16
VMEM_LIMIT = 56 * 1024 * 1024
TILE = 448
DEPTH = 3
RING = 4
PIECES = 4


def second_order(forward_sum, backward_sum, hidden_count):
    gate_value = forward_sum[:hidden_count]
    up_value = forward_sum[hidden_count : 2 * hidden_count]
    gate_tangent = forward_sum[2 * hidden_count : 3 * hidden_count]
    up_tangent = forward_sum[3 * hidden_count :]
    grad_hidden = backward_sum[:hidden_count]
    grad_tangent = backward_sum[hidden_count:]
    sigmoid_gate = jax.nn.sigmoid(gate_value)
    activation = gate_value * sigmoid_gate
    first_slope = sigmoid_gate * (1.0 + gate_value * (1.0 - sigmoid_gate))
    second_slope = (
        sigmoid_gate * (1.0 - sigmoid_gate) * (2.0 + gate_value * (1.0 - 2.0 * sigmoid_gate))
    )
    hidden_dot = first_slope * gate_tangent * up_value + activation * up_tangent
    gate_dot = (
        grad_tangent * up_value + grad_hidden * up_tangent
    ) * first_slope + grad_hidden * up_value * second_slope * gate_tangent
    up_dot = grad_tangent * activation + grad_hidden * first_slope * gate_tangent
    return jnp.concatenate((gate_dot, up_dot, hidden_dot), axis=0).astype(BF16)


def plain_shards(tokens, cotangent, gate_weight, up_weight, down_weight, gate_dir, up_dir, down_dir):
    hidden_count = gate_weight.shape[0]
    forward_stack = jnp.concatenate((gate_weight, up_weight, gate_dir, up_dir), axis=0)
    backward_stack = jnp.concatenate((down_weight, down_dir), axis=0)
    contract = (((1,), (1,)), ((), ()))
    token_rows = lax.all_gather(tokens, "row", axis=0, tiled=True)
    cot_rows = lax.all_gather(cotangent, "row", axis=0, tiled=True)
    forward_terms = lax.dot_general(forward_stack, token_rows, contract, preferred_element_type=F32)
    backward_terms = lax.dot_general(backward_stack, cot_rows, contract, preferred_element_type=F32)
    forward_sum, backward_sum = lax.psum((forward_terms, backward_terms), "col")
    results = second_order(forward_sum, backward_sum, hidden_count)
    paired = jnp.dot(results[: 2 * hidden_count], token_rows, preferred_element_type=F32)
    down_total = jnp.dot(results[2 * hidden_count :], cot_rows, preferred_element_type=F32)
    return (
        paired[:hidden_count].astype(BF16),
        paired[hidden_count:].astype(BF16),
        down_total.astype(BF16),
    )


def nt(a, b):
    return lax.dot_general(a, b, (((1,), (1,)), ((), ())), preferred_element_type=F32)


def slopes(products, extras, outs):
    gate_value, up_value, gate_tangent, up_tangent = products
    sigmoid = jax.nn.sigmoid(gate_value)
    rest = 1.0 - sigmoid
    activation = gate_value * sigmoid
    first = sigmoid * (1.0 + gate_value * rest)
    second = sigmoid * rest * (2.0 + gate_value * (1.0 - 2.0 * sigmoid))
    first_tangent = first * gate_tangent
    outs[0][...] = up_value * first
    outs[1][...] = up_tangent * first + up_value * (second * gate_tangent)
    outs[2][...] = activation
    outs[3][...] = first_tangent
    outs[4][...] = (first_tangent * up_value + activation * up_tangent).astype(BF16)


def combine(products, extras, outs):
    grad_hidden, grad_tangent = products
    outs[0][...] = (grad_tangent * extras[0][...] + grad_hidden * extras[1][...]).astype(BF16)
    outs[1][...] = (grad_tangent * extras[2][...] + grad_hidden * extras[3][...]).astype(BF16)


def products_kernel(epilogue, own, far, slots, far_slots, extras, outs, scratch):
    bufs, rows, sems = scratch
    step, steps = pl.program_id(0), pl.num_programs(0)
    tiles = [side[p] for p in range(len(own)) for side in (own, far)]
    count = len(tiles)
    piece = TILE // PIECES

    def start(at, index):
        ref, first = tiles[index]
        for i in range(PIECES):
            row = pl.multiple_of(first + at * TILE + i * piece, 16)
            pltpu.make_async_copy(
                ref.at[pl.ds(row, piece), :],
                bufs.at[index % RING, pl.ds(i * piece, piece), :],
                sems.at[index % RING],
            ).start()

    @pl.when(step == 0)
    def _():
        for index in range(DEPTH):
            start(0, index)
        for side, refs in ((0, slots), (1, far_slots)):
            at = 0
            for ref in refs:
                rows[side, at : at + ref.shape[0], :] = ref[...]
                at += ref.shape[0]

    products, total = [], None
    for index in range(count):
        ahead = index + DEPTH
        if ahead < count:
            start(step, ahead)
        else:

            @pl.when(step + 1 < steps)
            def _():
                start(step + 1, ahead - count)

        buf = bufs.at[index % RING]
        pltpu.make_async_copy(buf, buf, sems.at[index % RING]).wait()
        part = nt(buf[...], rows[index % 2])
        if index % 2 == 0:
            total = part
        else:
            products.append(total + part)
    epilogue(products, extras, outs)


def products_call(
    name, epilogue, core, own, far, slots, far_slots, extras, out_types, part=None, into=()
):
    features = own[0].shape[1]
    hidden = own[0].shape[0] // 2
    count = sum(slot.shape[0] for slot in slots)
    far_arrays = []
    for array, _ in far:
        if not any(array is other for other in far_arrays):
            far_arrays.append(array)
    places = [
        ([array is other for other in far_arrays].index(True), which * hidden)
        for array, which in far
    ]
    n_own, n_far, n_slots, n_side = len(own), len(far_arrays), len(slots), len(far_slots)
    base, tiles = (0, hidden // TILE) if part is None else part

    def kernel(core_ref, *refs):
        refs = list(refs)

        def take(n):
            taken, refs[:] = refs[:n], refs[n:]
            return taken

        own_refs, far_refs = take(n_own), take(n_far)
        slot_refs, side_refs = take(n_slots), take(n_side)
        extra_refs, _, out_refs = take(len(extras)), take(len(into)), take(len(out_types))
        products_kernel(
            epilogue,
            [(ref, core_ref[0] * hidden + base * TILE) for ref in own_refs],
            [(far_refs[i], first + base * TILE) for i, first in places],
            slot_refs,
            side_refs,
            extra_refs,
            out_refs,
            refs,
        )

    block = pl.BlockSpec((TILE, count), lambda i, c: (i + base, 0))
    whole = [pl.BlockSpec(a.shape, lambda i, c: (0, 0)) for a in (*slots, *far_slots)]
    done = tiles * TILE
    moved = 4 * len(own) * done * features + done * count * (
        4 * len(extras) + sum(jnp.dtype(t).itemsize for t in out_types)
    )
    return pl.pallas_call(
        kernel,
        out_shape=[jax.ShapeDtypeStruct((hidden, count), t) for t in out_types],
        grid_spec=pltpu.PrefetchScalarGridSpec(
            num_scalar_prefetch=1,
            grid=(tiles,),
            in_specs=[pl.BlockSpec(memory_space=pl.ANY)] * (n_own + n_far)
            + whole
            + [block] * len(extras)
            + [pl.BlockSpec(memory_space=pl.ANY)] * len(into),
            out_specs=[block] * len(out_types),
            scratch_shapes=[
                pltpu.VMEM((RING, TILE, features), BF16),
                pltpu.VMEM((2, count, features), BF16),
                pltpu.SemaphoreType.DMA((RING,)),
            ],
        ),
        compiler_params=pltpu.CompilerParams(vmem_limit_bytes=VMEM_LIMIT),
        cost_estimate=pl.CostEstimate(
            flops=4 * len(own) * done * features * count,
            bytes_accessed=moved,
            transcendentals=0,
        ),
        input_output_aliases={
            1 + n_own + n_far + n_slots + n_side + len(extras) + i: i for i in range(len(into))
        },
        name=name,
    )(core, *own, *far_arrays, *slots, *far_slots, *extras, *into)


def outer_call(name, core, products, slots):
    n_prod, n_chunks = len(products), len(products[0][0])
    half, count = products[0][0][0].shape
    features = slots[0].shape[1]
    depth = n_chunks * count
    tiles = half // TILE
    own = [chunk for pair in products for chunk in pair[0]]
    far = [chunk for pair in products for chunk in pair[1]]

    def kernel(core_ref, *refs):
        own_refs, refs = refs[: len(own)], refs[len(own) :]
        far_refs, refs = refs[: len(far)], refs[len(far) :]
        slot_refs, refs = refs[: len(slots)], refs[len(slots) :]
        outs, rows = refs[:-1], refs[-1]
        step = pl.program_id(0)

        @pl.when(step == 0)
        def _():
            at = 0
            for ref in slot_refs:
                rows[at : at + ref.shape[0], :] = ref[...]
                at += ref.shape[0]

        def work(refs):
            for prod in range(n_prod):
                chunks = refs[prod * n_chunks : (prod + 1) * n_chunks]
                left = jnp.concatenate([ref[...] for ref in chunks], axis=1)
                outs[prod][...] = jnp.dot(
                    left, rows[...], preferred_element_type=F32
                ).astype(BF16)

        pl.when(step < tiles)(lambda: work(own_refs))
        pl.when(step >= tiles)(lambda: work(far_refs))

    def place(i, c):
        return (jnp.where(i < tiles, c[0] * tiles + i, (1 - c[0]) * tiles + i - tiles), 0)

    return pl.pallas_call(
        kernel,
        out_shape=[jax.ShapeDtypeStruct((2 * half, features), BF16)] * n_prod,
        grid_spec=pltpu.PrefetchScalarGridSpec(
            num_scalar_prefetch=1,
            grid=(2 * tiles,),
            in_specs=[
                pl.BlockSpec((TILE, count), lambda i, c: (jnp.minimum(i, tiles - 1), 0))
            ] * len(own)
            + [
                pl.BlockSpec((TILE, count), lambda i, c: (jnp.maximum(i - tiles, 0), 0))
            ] * len(far)
            + [pl.BlockSpec(slot.shape, lambda i, c: (0, 0)) for slot in slots],
            out_specs=[pl.BlockSpec((TILE, features), place)] * n_prod,
            scratch_shapes=[pltpu.VMEM((depth, features), BF16)],
        ),
        compiler_params=pltpu.CompilerParams(vmem_limit_bytes=VMEM_LIMIT),
        cost_estimate=pl.CostEstimate(
            flops=4 * n_prod * half * features * depth,
            bytes_accessed=2 * (2 * n_prod * half * (features + depth) + depth * features),
            transcendentals=0,
        ),
        name=name,
    )(core, *own, *far, *slots)


def line_pairs(pairs):
    return [(2 * a + x, 2 * b + x) for a, b in pairs for x in range(2)]


X_SWAP = [(r, r ^ 1) for r in range(8)]
X_ENDS = [(r, r ^ 1) for r in (0, 1, 6, 7)]
OUTER = line_pairs([(0, 1), (1, 0), (2, 3), (3, 2)])
OUTWARD = line_pairs([(1, 0), (2, 3)])
INNER = line_pairs([(1, 2), (2, 1)])


def send(value, pairs):
    return lax.ppermute(value, "row", pairs)


def core_swap(*values):
    value = values[0] if len(values) == 1 else jnp.concatenate(values, axis=0)
    return lax.ppermute(value, "col", [(0, 1), (1, 0)])


def tie(*values):
    return lax.optimization_barrier(values)


def shards(tokens, cotangent, gate_weight, up_weight, down_weight, gate_dir, up_dir, down_dir):
    core = lax.axis_index("col")
    line = lax.axis_index("row") // 2
    inner = (line == 1) | (line == 2)
    half = gate_weight.shape[0] // 2
    here = core.reshape(1).astype(jnp.int32)

    def pick(a, b):
        return jnp.where(inner, a, b)

    def lend(*weights):
        return core_swap(
            *[lax.dynamic_slice_in_dim(w, (1 - core) * half, half, 0) for w in weights]
        )

    t0, c0 = tokens, cotangent
    ta1, tb1, tx1 = send(t0, OUTER), send(t0, INNER), send(t0, X_SWAP)
    gate_far = lend(gate_weight)
    gate_dir_far = lend(gate_dir)
    t0, ta1, tb1, tx1, gate_far, gate_dir_far, up_weight, up_dir = tie(
        t0, ta1, tb1, tx1, gate_far, gate_dir_far, up_weight, up_dir
    )
    ta2, tb2, tx2 = send(tb1, OUTWARD), send(ta1, INNER), send(ta1, X_SWAP)
    up_far = lend(up_weight)
    up_dir_far = lend(up_dir)
    ts2 = pick(tb1, ta2)
    c0, ts2, tb2, tx2, up_far, up_dir_far = tie(c0, ts2, tb2, tx2, up_far, up_dir_far)
    t_far1 = core_swap(t0, ta1, tx1, tx2)
    ta3, tx3 = send(tb2, OUTWARD), send(ts2, X_SWAP)
    ca1, cb1, cx1 = send(c0, OUTER), send(c0, INNER), send(c0, X_SWAP)

    def forward(name, slots, far_slots, part=None, into=()):
        return products_call(
            name, slopes, here,
            [gate_weight, up_weight, gate_dir, up_dir],
            [(gate_far, 0), (up_far, 0), (gate_dir_far, 0), (up_dir_far, 0)],
            slots, far_slots, [], [F32] * 4 + [BF16], part, into,
        )

    def backward(name, slots, far_slots, coefs):
        return products_call(
            name, combine, here,
            [down_weight, down_dir], [(down_far, 0), (down_dir_far, 0)],
            slots, far_slots, coefs, [BF16, BF16],
        )

    first = forward("forward1", [t0, ta1, tx1, tx2], [t_far1])
    ts3 = pick(tb2, ta3)
    ts3, tx3, ca1, cb1, cx1, first, down_weight, down_dir = tie(
        ts3, tx3, ca1, cb1, cx1, first, down_weight, down_dir
    )
    down_far, down_dir_far = lend(down_weight), lend(down_dir)
    tx4 = send(ts3, X_SWAP)
    ca2, cb2 = send(pick(cb1, cx1), OUTER), send(ca1, INNER)
    tx4, ca2, cb2, down_far, down_dir_far = tie(tx4, ca2, cb2, down_far, down_dir_far)
    t_far2 = core_swap(ts2, ts3, tx3, tx4)
    cx2, ca3, cb3 = send(pick(cb1, ca1), X_SWAP), send(cb2, OUTWARD), send(ca2, INNER)
    slots2 = [ts2, ts3, tx3, tx4]
    second = forward("forward2a", slots2, [t_far2], (0, 1))
    cx2, ca3, cb3, second, t_far2 = tie(cx2, ca3, cb3, second, t_far2)
    cs2, cs3, cs5 = pick(cb1, ca2), pick(cb2, ca3), pick(ca2, cx2)
    cx3, ca4 = send(ca2, X_ENDS), send(cb3, OUTWARD)
    *coefs1, hidden1 = first
    hidden_far1 = core_swap(hidden1)
    c_far1 = core_swap(c0, ca1, cx1, cs5)
    *coefs2, hidden2 = forward("forward2b", slots2, [t_far2], (1, half // TILE - 1), second)
    cx3, ca4, hidden_far1, c_far1, coefs2, hidden2 = tie(
        cx3, ca4, hidden_far1, c_far1, coefs2, hidden2
    )
    cs6, cs7 = pick(cx2, cx3), pick(cb3, ca4)
    c_far2 = core_swap(cs2, cs3, cs6, cs7)
    hidden_far2 = core_swap(hidden2)
    gate1, up1 = backward("backward1", [c0, ca1, cx1, cs5], [c_far1], coefs1)
    c_far2, hidden_far2, gate1, up1 = tie(c_far2, hidden_far2, gate1, up1)
    gate_far1, up_far1 = core_swap(gate1), core_swap(up1)
    gate2, up2 = backward("backward2", [cs2, cs3, cs6, cs7], [c_far2], coefs2)
    gate2, up2, gate_far1, up_far1 = tie(gate2, up2, gate_far1, up_far1)
    gate_far2, up_far2 = core_swap(gate2), core_swap(up2)
    (hvp_down,) = outer_call(
        "hvp_down", here,
        [([hidden1, hidden2], [hidden_far1, hidden_far2])],
        [c0, ca1, cx1, cs5, cs2, cs3, cs6, cs7],
    )
    hvp_down, gate_far2, up_far2 = tie(hvp_down, gate_far2, up_far2)
    hvp_gate, hvp_up = outer_call(
        "hvp_pair", here,
        [
            ([gate1, gate2], [gate_far1, gate_far2]),
            ([up1, up2], [up_far1, up_far2]),
        ],
        [t0, ta1, tx1, tx2, ts2, ts3, tx3, tx4],
    )
    return (hvp_gate, hvp_up, hvp_down)


def solution(mesh):
    in_specs = (P(("groups", "row"), "col"),) * 2 + (P("row", "col"),) * 6
    out_specs = (P(("groups", "row"), "col"),) * 3

    def run(tokens, cotangent, *weights):
        rows, cols = mesh.shape["row"], mesh.shape["col"]
        block = tokens.shape[0] // (mesh.shape["groups"] * rows)
        hidden = weights[0].shape[0] // rows
        features = tokens.shape[1] // cols
        fits = (
            rows == 8 and cols == 2 and block % 128 == 0
            and hidden % (2 * TILE) == 0 and features % 128 == 0
        )
        body = shards if fits else plain_shards
        return jax.shard_map(
            body, mesh=mesh, in_specs=in_specs, out_specs=out_specs, check_vma=False
        )(tokens, cotangent, *weights)

    return run
```

time: 417 us -> 245 us (0.59)
  waiting for transfers between devices: 258 us -> 41.3 us
  Pallas kernels: 0 us -> 126 us
  matrix products: 113 us -> 0 us
  starting transfers between devices: 0.11 us -> 43.2 us
  between operations: 13.7 us -> 1.5 us
  other arithmetic: 19.4 us -> 13.1 us
  local copies, waits for them, and re-layouts: 11.1 us -> 17.1 us
    psum x1 -> x0, waiting for transfers between devices: 131 us -> none  [shards(): forward_sum, backward_sum = lax.psum((forward_terms, backward_terms), 'col')]
    all_gather x2 -> x0, waiting for transfers between devices: 126 us -> none  [the longest x1 74.3 us: shards(): cot_rows = lax.all_gather(cotangent, 'row', axis=0, tiled=True)]
    pallas_call x0 -> x7, Pallas kernels: none -> 126 us  [the longest x5 90.8 us: products_call(): pl.pallas_call(kernel, out_shape=[jax.ShapeDtypeStruct((hidden, count), t...]
    dot_general x4 -> x0, matrix products: 113 us -> none  [the longest x1 50.4 us: shards(): lax.dot_general(forward_stack, token_rows, contract, preferred_element_ty...]
    ppermute x0 -> x35, starting transfers between devices: none -> 43.2 us  [the longest x19 32.8 us: send(): return lax.ppermute(value, 'row', pairs)]
    ppermute x0 -> x35, waiting for transfers between devices: none -> 41.3 us  [the longest x19 41.3 us: send(): return lax.ppermute(value, 'row', pairs)]
    another operation x1 -> x0, other arithmetic: 19.4 us -> none
    slice x1 -> x0, local copies, waits for them, and re-layouts: 11.1 us -> none  [shards(): hvp_up = paired[hidden_count:].astype(jnp.bfloat16)]
  transfers between devices with their start and end apart: 3 -> 35, of which waited for: 3 -> 9; matrix products, arithmetic and copies ran while one was open for 5% -> 4% of each run, Pallas kernels for 0% -> 43%
where the time goes in v1:
time: 245 us; the launch traced here: 242 us
  Pallas kernels  126 us (51%)
  starting transfers between devices  43.2 us (18%)
  waiting for transfers between devices  41.3 us (17%)
  local copies, waits for them, and re-layouts  17.1 us (7%)
  other arithmetic  13.1 us (5%)
    pallas_call x5, Pallas kernels, products_call(): pl.pallas_call(kernel, out_shape=[jax.ShapeDtypeStruct((hidden, count), t...  90.8 us
    ppermute x19, waiting for transfers between devices, send(): return lax.ppermute(value, 'row', pairs)  41.3 us
    pallas_call x2, Pallas kernels, outer_call(): pl.pallas_call(kernel, out_shape=[jax.ShapeDtypeStruct((2 * half, feature...  34.9 us
    ppermute x19, starting transfers between devices, send(): return lax.ppermute(value, 'row', pairs)  32.8 us
    dynamic_slice x6, local copies, waits for them, and re-layouts, lend(): lax.dynamic_slice_in_dim(w, (1 - core) * half, half, 0)  11 us
    ppermute x16, starting transfers between devices, core_swap(): return lax.ppermute(value, 'col', [(0, 1), (1, 0)])  10.3 us
    select_n x6, other arithmetic, pick(): return jnp.where(inner, a, b)  6.64 us
    concatenate x4, other arithmetic, core_swap(): value = values[0] if len(values) == 1 else jnp.concatenate(values, axis=0)  6.44 us
  transfers between devices with their start and end apart: 35, of which 9 were waited for; matrix products, arithmetic and copies ran while one was open for 4% of the time, Pallas kernels for 43%

profile of v1, /device:TPU:13, one launch (start us, length us, event | category | flops | bytes accessed | tf_op | source)
XLA Modules:
  0.0 241.9 jit_solution(8905965816071171561)
XLA Ops:
  0.6 2.6 %constant_dynamic-slice_fusion.5 = bf16[896,2048]{1,0:T(8,128)(2,1)S(1)} fusion(bf16[1792,2048]{1,0:T(8,128)(2,1)} %refs_0_.5, s32[]{:T(128)S(6)} %select_n.55), kind=kLoop, calls=%fused_computation.18 | loop fusion | bytes 7340036 | tf_op jit(solution)/shard_map/dynamic_slice | solution.py:304
  6.3 4.5 %collective-permute-start.1 = (bf16[128,2048]{1,0:T(8,128)(2,1)}, bf16[128,2048]{1,0:T(8,128)(2,1)S(1)}, u32[]{:S(2)}, u32[]{:S(2)}) collective-permute-start(bf16[128,2048]{1,0:T(8,128)(2,1)} %refs_8_.1), channel_id=1, source_target_pairs={{4,8},{6,10},{8,4},{10,6},{5,9},{7,11},{9,5},{11,7},{20,24},{22,26... | collective-permute-start | bytes 1572872 | tf_op jit(solution)/shard_map/ppermute | solution.py:280
  12.0 7.8 %collective-permute-done.refs_9_ = bf16[128,2048]{1,0:T(8,128)(2,1)S(1)} collective-permute-done((bf16[128,2048]{1,0:T(8,128)(2,1)}, bf16[128,2048]{1,0:T(8,128)(2,1)S(1)}, u32[]{:S(2)}, u32[]{:S(2)}) %collective-permute-start) | collective-permute-done | bytes 524320 | tf_op jit(solution)/shard_map/ppermute | solution.py:280
  19.8 3.0 %collective-permute-done.1 = bf16[128,2048]{1,0:T(8,128)(2,1)S(1)} collective-permute-done((bf16[128,2048]{1,0:T(8,128)(2,1)}, bf16[128,2048]{1,0:T(8,128)(2,1)S(1)}, u32[]{:S(2)}, u32[]{:S(2)}) %collective-permute-start.1) | collective-permute-done | bytes 524320 | tf_op jit(solution)/shard_map/ppermute | solution.py:280
  23.7 2.7 %constant_dynamic-slice_fusion.3 = bf16[896,2048]{1,0:T(8,128)(2,1)} fusion(bf16[1792,2048]{1,0:T(8,128)(2,1)S(1)} %copy-done, s32[]{:T(128)S(6)} %select_n.55), kind=kLoop, calls=%fused_computation.16 | loop fusion | bytes 7340036 | tf_op jit(solution)/shard_map/dynamic_slice | solution.py:304
  26.6 1.6 collective-permute-start.8
  28.3 2.3 constant_dynamic-slice_fusion.2
  31.9 1.9 collective-permute-start.6
  35.1 7.8 %collective-permute-done.5 = bf16[128,2048]{1,0:T(8,128)(2,1)S(1)} collective-permute-done((bf16[128,2048]{1,0:T(8,128)(2,1)S(1)}, bf16[128,2048]{1,0:T(8,128)(2,1)S(1)}, u32[]{:S(2)}, u32[]{:S(2)}) %collective-permute-start.5) | collective-permute-done | bytes 524320 | tf_op jit(solution)/shard_map/ppermute | solution.py:280
  43.0 3.9 %collective-permute-done.6 = bf16[128,2048]{1,0:T(8,128)(2,1)S(1)} collective-permute-done((bf16[128,2048]{1,0:T(8,128)(2,1)S(1)}, bf16[128,2048]{1,0:T(8,128)(2,1)S(1)}, u32[]{:S(2)}, u32[]{:S(2)}) %collective-permute-start.6) | collective-permute-done | bytes 524320 | tf_op jit(solution)/shard_map/ppermute | solution.py:280
  48.1 1.5 collective-permute-start.15
  51.0 3.5 %collective-permute-start.13 = (bf16[128,2048]{1,0:T(8,128)(2,1)}, bf16[128,2048]{1,0:T(8,128)(2,1)}, u32[]{:S(2)}, u32[]{:S(2)}) collective-permute-start(bf16[128,2048]{1,0:T(8,128)(2,1)} %refs_4_.1), channel_id=1, source_target_pairs={{4,8},{6,10},{8,4},{10,6},{5,9},{7,11},{9,5},{11,7},{20,24},{22,26... | collective-permute-start | bytes 1572872 | tf_op jit(solution)/shard_map/ppermute | solution.py:280
  55.9 6.6 %collective-permute-done.10 = bf16[128,2048]{1,0:T(8,128)(2,1)S(1)} collective-permute-done((bf16[128,2048]{1,0:T(8,128)(2,1)S(1)}, bf16[128,2048]{1,0:T(8,128)(2,1)S(1)}, u32[]{:S(2)}, u32[]{:S(2)}) %collective-permute-start.10) | collective-permute-done | bytes 524320 | tf_op jit(solution)/shard_map/ppermute | solution.py:280
  65.9 26.5 %forward1.1 = (f32[896,512]{1,0:T(8,128)}, f32[896,512]{1,0:T(8,128)}, f32[896,512]{1,0:T(8,128)}, f32[896,512]{1,0:T(8,128)}, bf16[896,512]{1,0:T(8,128)(2,1)}) custom-call(s32[1]{0:T(128)} %bitcast.core_ref, bf16[1792,2048]{1,0:T(8,128)(2,1)} %refs_0_.5, bf16[1792,2048]{1,0:T(8,128)(2,1)} %refs_1_.2, bf16[1792,2048]{1,0:T(8,128)(2,1)} %refs_2_.5, ...), custom_call_target="tpu_custom_call" | custom-call | flops 15032385536 | bytes 37617664 | tf_op jit(solution)/shard_map/forward1/pallas_call | solution.py:175
  94.0 2.5 %constant_dynamic-slice_fusion = bf16[896,2048]{1,0:T(8,128)(2,1)S(1)} fusion(bf16[1792,2048]{1,0:T(8,128)(2,1)} %refs_1_.4, s32[]{:T(128)S(6)} %select_n.55), kind=kLoop, calls=%fused_computation.13 | loop fusion | bytes 7340036 | tf_op jit(solution)/shard_map/dynamic_slice | solution.py:304
  96.6 1.9 broadcast_select_fusion.6
  98.6 2.5 %collective-permute-start.17 = (bf16[128,2048]{1,0:T(8,128)(2,1)S(1)}, bf16[128,2048]{1,0:T(8,128)(2,1)}, u32[]{:S(2)}, u32[]{:S(2)}) collective-permute-start(bf16[128,2048]{1,0:T(8,128)(2,1)S(1)} %get-tuple-element.167), channel_id=1, source_target_pairs={{0,4},{2,6},{4,0},{6,2},{8,12},{10,14},{12,8},{14,10},{1,5},{3,7},... | collective-permute-start | bytes 1572872 | tf_op jit(solution)/shard_map/ppermute | solution.py:280
  101.3 3.4 %collective-permute-start.18 = (bf16[128,2048]{1,0:T(8,128)(2,1)}, bf16[128,2048]{1,0:T(8,128)(2,1)}, u32[]{:S(2)}, u32[]{:S(2)}) collective-permute-start(bf16[128,2048]{1,0:T(8,128)(2,1)} %collective-permute-done.12.refs_5_), channel_id=1, source_target_pairs={{4,8},{6,10},{8,4},{10,6},{5,9},{7,11},{9,5},{11,7},{20,24},{22,26... | collective-permute-start | bytes 1572872 | tf_op jit(solution)/shard_map/ppermute | solution.py:280
  104.7 8.4 %collective-permute-done.17 = bf16[128,2048]{1,0:T(8,128)(2,1)} collective-permute-done((bf16[128,2048]{1,0:T(8,128)(2,1)S(1)}, bf16[128,2048]{1,0:T(8,128)(2,1)}, u32[]{:S(2)}, u32[]{:S(2)}) %collective-permute-start.17) | collective-permute-done | bytes 524320 | tf_op jit(solution)/shard_map/ppermute | solution.py:280
  113.9 2.0 collective-permute-done.18
  116.0 1.7 pad_maximum_fusion.1
  117.7 2.0 collective-permute-start.24
  120.9 2.1 collective-permute-start.22
  123.0 3.5 %collective-permute-start.23 = (bf16[128,2048]{1,0:T(8,128)(2,1)}, bf16[128,2048]{1,0:T(8,128)(2,1)}, u32[]{:S(2)}, u32[]{:S(2)}) collective-permute-start(bf16[128,2048]{1,0:T(8,128)(2,1)} %collective-permute-done.17), channel_id=1, source_target_pairs={{4,8},{6,10},{8,4},{10,6},{5,9},{7,11},{9,5},{11,7},{20,24},{22,26... | collective-permute-start | bytes 1572872 | tf_op jit(solution)/shard_map/ppermute | solution.py:280
  126.5 15.6 %forward2a.1 = (f32[896,512]{1,0:T(8,128)}, f32[896,512]{1,0:T(8,128)}, f32[896,512]{1,0:T(8,128)}, f32[896,512]{1,0:T(8,128)}, bf16[896,512]{1,0:T(8,128)(2,1)}) custom-call(s32[1]{0:T(128)} %bitcast.core_ref, bf16[1792,2048]{1,0:T(8,128)(2,1)} %refs_0_.5, bf16[1792,2048]{1,0:T(8,128)(2,1)} %refs_1_.2, bf16[1792,2048]{1,0:T(8,128)(2,1)} %refs_2_.5, ...), custom_call_target="tpu_custom_call" | custom-call | flops 7516192768 | bytes 18808832 | tf_op jit(solution)/shard_map/forward2a/pallas_call | solution.py:175
  143.5 2.0 pad_maximum_fusion.2
  148.3 15.6 %forward2b.1 = (f32[896,512]{1,0:T(8,128)}, f32[896,512]{1,0:T(8,128)}, f32[896,512]{1,0:T(8,128)}, f32[896,512]{1,0:T(8,128)}, bf16[896,512]{1,0:T(8,128)(2,1)}) custom-call(s32[1]{0:T(128)} %bitcast.core_ref, bf16[1792,2048]{1,0:T(8,128)(2,1)} %refs_0_.5, ...), custom_call_target="tpu_custom_call", output_to_operand_aliasing={{0}: (14, {}), {1}: (15, {}), {2}: (16, {}), {3}: (17, {}),... | custom-call | flops 7516192768 | bytes 18808832 | tf_op jit(solution)/shard_map/forward2b/pallas_call | solution.py:175
  167.4 1.6 pad_maximum_fusion.3
  169.5 16.8 %backward1.1 = (bf16[896,512]{1,0:T(8,128)(2,1)}, bf16[896,512]{1,0:T(8,128)(2,1)}) custom-call(s32[1]{0:T(128)} %bitcast.core_ref, bf16[1792,2048]{1,0:T(8,128)(2,1)} %refs_0_.7, bf16[1792,2048]{1,0:T(8,128)(2,1)} %refs_1_.4, bf16[896,2048]{1,0:T(8,128)(2,1)} %copy-done.4, bf16[896,2048]{1,0:T(8,128)(2,1)} %copy-done.5, bf16[128,2048]{1,0:T(8,128)(2,1)} %refs_4_.1, ...), custom_call_target="tpu_custom_call" | custom-call | flops 7516192768 | bytes 23855104 | tf_op jit(solution)/shard_map/backward1/pallas_call | solution.py:175
  187.7 16.4 %backward2.1 = (bf16[896,512]{1,0:T(8,128)(2,1)}, bf16[896,512]{1,0:T(8,128)(2,1)}) custom-call(s32[1]{0:T(128)} %bitcast.core_ref, bf16[1792,2048]{1,0:T(8,128)(2,1)} %refs_0_.7, bf16[1792,2048]{1,0:T(8,128)(2,1)} %refs_1_.4, bf16[896,2048]{1,0:T(8,128)(2,1)} %copy-done.4, bf16[896,2048]{1,0:T(8,128)(2,1)} %copy-done.5, bf16[128,2048]{1,0:T(8,128)(2,1)} %copy-done.10, ...), custom_call_target="tpu_custom_call" | custom-call | flops 7516192768 | bytes 23855104 | tf_op jit(solution)/shard_map/backward2/pallas_call | solution.py:175
  204.7 12.9 %hvp_down.1 = bf16[1792,2048]{1,0:T(8,128)(2,1)} custom-call(s32[1]{0:T(128)} %bitcast.core_ref, bf16[896,512]{1,0:T(8,128)(2,1)} %get-tuple-element.121.refs_0_, bf16[896,512]{1,0:T(8,128)(2,1)} %get-tuple-element.135.refs_1_, bf16[896,512]{1,0:T(8,128)(2,1)} %copy-done.21, bf16[896,512]{1,0:T(8,128)(2,1)} %copy-done.22, bf16[128,2048]{1,0:T(8,128)(2,1)} %refs_4_.1, ...), custom_call_target="tpu_custom_call" | custom-call | flops 7516192768 | bytes 15204352 | tf_op jit(solution)/shard_map/hvp_down/pallas_call | solution.py:242
  219.6 22.0 %hvp_pair.1 = (bf16[1792,2048]{1,0:T(8,128)(2,1)}, bf16[1792,2048]{1,0:T(8,128)(2,1)}) custom-call(s32[1]{0:T(128)} %bitcast.core_ref, bf16[896,512]{1,0:T(8,128)(2,1)} %get-tuple-element.145.refs_0_, bf16[896,512]{1,0:T(8,128)(2,1)} %get-tuple-element.154.refs_1_, bf16[896,512]{1,0:T(8,128)(2,1)} %get-tuple-element.153.refs_2_, ...), custom_call_target="tpu_custom_call" | custom-call | flops 15032385536 | bytes 26214400 | tf_op jit(solution)/shard_map/hvp_pair/pallas_call | solution.py:242
  (120 shorter events, 31.4 us)
Async XLA Ops:
  3.3 20.4 %collective-permute-start.3 = (bf16[896,2048]{1,0:T(8,128)(2,1)S(1)}, bf16[896,2048]{1,0:T(8,128)(2,1)S(1)}, u32[]{:S(2)}, u32[]{:S(2)}) collective-permute-start(bf16[896,2048]{1,0:T(8,128)(2,1)S(1)} %constant_dynamic-slice_fusion.5), channel_id=1, source_target_pairs={{0,1},{1,0},{2,3},{3,2},{4,5},{5,4},{6,7},{7,6},{8,9},{9,8},{10,11... | collective-permute-start | bytes 11010056 | tf_op jit(solution)/shard_map/ppermute | solution.py:285
  5.3 18.4 %collective-permute-start.4 = (bf16[896,2048]{1,0:T(8,128)(2,1)S(1)}, bf16[896,2048]{1,0:T(8,128)(2,1)}, u32[]{:S(2)}, u32[]{:S(2)}) collective-permute-start(bf16[896,2048]{1,0:T(8,128)(2,1)S(1)} %constant_dynamic-slice_fusion.4), channel_id=1, source_target_pairs={{0,1},{1,0},{2,3},{3,2},{4,5},{5,4},{6,7},{7,6},{8,9},{9,8},{10,11... | collective-permute-start | bytes 11010056 | tf_op jit(solution)/shard_map/ppermute | solution.py:285
  6.1 13.7 %collective-permute-start = (bf16[128,2048]{1,0:T(8,128)(2,1)}, bf16[128,2048]{1,0:T(8,128)(2,1)S(1)}, u32[]{:S(2)}, u32[]{:S(2)}) collective-permute-start(bf16[128,2048]{1,0:T(8,128)(2,1)} %refs_8_.1), channel_id=1, source_target_pairs={{0,4},{2,6},{4,0},{6,2},{8,12},{10,14},{12,8},{14,10},{1,5},{3,7},... | collective-permute-start | bytes 1572872 | tf_op jit(solution)/shard_map/ppermute | solution.py:280
  6.3 16.5 %collective-permute-start.1 = (bf16[128,2048]{1,0:T(8,128)(2,1)}, bf16[128,2048]{1,0:T(8,128)(2,1)S(1)}, u32[]{:S(2)}, u32[]{:S(2)}) collective-permute-start(bf16[128,2048]{1,0:T(8,128)(2,1)} %refs_8_.1), channel_id=1, source_target_pairs={{4,8},{6,10},{8,4},{10,6},{5,9},{7,11},{9,5},{11,7},{20,24},{22,26... | collective-permute-start | bytes 1572872 | tf_op jit(solution)/shard_map/ppermute | solution.py:280
  10.7 13.0 %collective-permute-start.2 = (bf16[128,2048]{1,0:T(8,128)(2,1)}, bf16[128,2048]{1,0:T(8,128)(2,1)S(1)}, u32[]{:S(2)}, u32[]{:S(2)}) collective-permute-start(bf16[128,2048]{1,0:T(8,128)(2,1)} %refs_8_.1), channel_id=1, source_target_pairs={{0,2},{2,0},{4,6},{6,4},{8,10},{10,8},{12,14},{14,12},{1,3},{3,1},... | collective-permute-start | bytes 1572872 | tf_op jit(solution)/shard_map/ppermute | solution.py:280
  26.6 20.2 %collective-permute-start.8 = (bf16[896,2048]{1,0:T(8,128)(2,1)}, bf16[896,2048]{1,0:T(8,128)(2,1)}, u32[]{:S(2)}, u32[]{:S(2)}) collective-permute-start(bf16[896,2048]{1,0:T(8,128)(2,1)} %constant_dynamic-slice_fusion.3), channel_id=1, source_target_pairs={{0,1},{1,0},{2,3},{3,2},{4,5},{5,4},{6,7},{7,6},{8,9},{9,8},{10,11... | collective-permute-start | bytes 11010056 | tf_op jit(solution)/shard_map/ppermute | solution.py:285
  30.6 16.3 %collective-permute-start.9 = (bf16[896,2048]{1,0:T(8,128)(2,1)}, bf16[896,2048]{1,0:T(8,128)(2,1)}, u32[]{:S(2)}, u32[]{:S(2)}) collective-permute-start(bf16[896,2048]{1,0:T(8,128)(2,1)} %constant_dynamic-slice_fusion.2), channel_id=1, source_target_pairs={{0,1},{1,0},{2,3},{3,2},{4,5},{5,4},{6,7},{7,6},{8,9},{9,8},{10,11... | collective-permute-start | bytes 11010056 | tf_op jit(solution)/shard_map/ppermute | solution.py:285
  31.9 15.0 %collective-permute-start.6 = (bf16[128,2048]{1,0:T(8,128)(2,1)S(1)}, bf16[128,2048]{1,0:T(8,128)(2,1)S(1)}, u32[]{:S(2)}, u32[]{:S(2)}) collective-permute-start(bf16[128,2048]{1,0:T(8,128)(2,1)S(1)} %collective-permute-done.refs_9_), channel_id=1, source_target_pairs={{4,8},{6,10},{8,4},{10,6},{5,9},{7,11},{9,5},{11,7},{20,24},{22,26... | collective-permute-start | bytes 1572872 | tf_op jit(solution)/shard_map/ppermute | solution.py:280
  33.8 13.1 %collective-permute-start.7 = (bf16[128,2048]{1,0:T(8,128)(2,1)S(1)}, bf16[128,2048]{1,0:T(8,128)(2,1)}, u32[]{:S(2)}, u32[]{:S(2)}) collective-permute-start(bf16[128,2048]{1,0:T(8,128)(2,1)S(1)} %collective-permute-done.refs_9_), channel_id=1, source_target_pairs={{0,2},{2,0},{4,6},{6,4},{8,10},{10,8},{12,14},{14,12},{1,3},{3,1},... | collective-permute-start | bytes 1572872 | tf_op jit(solution)/shard_map/ppermute | solution.py:280
  48.1 16.4 %collective-permute-start.15 = (bf16[512,2048]{1,0:T(8,128)(2,1)S(1)}, bf16[512,2048]{1,0:T(8,128)(2,1)S(1)}, u32[]{:S(2)}, u32[]{:S(2)}) collective-permute-start(bf16[512,2048]{1,0:T(8,128)(2,1)S(1)} %pad_maximum_fusion), channel_id=1, source_target_pairs={{0,1},{1,0},{2,3},{3,2},{4,5},{5,4},{6,7},{7,6},{8,9},{9,8},{10,11... | collective-permute-start | bytes 6291464 | tf_op jit(solution)/shard_map/ppermute | solution.py:285
  51.0 41.4 %collective-permute-start.12 = (bf16[128,2048]{1,0:T(8,128)(2,1)}, bf16[128,2048]{1,0:T(8,128)(2,1)}, u32[]{:S(2)}, u32[]{:S(2)}) collective-permute-start(bf16[128,2048]{1,0:T(8,128)(2,1)} %refs_4_.1), channel_id=1, source_target_pairs={{0,4},{2,6},{4,0},{6,2},{8,12},{10,14},{12,8},{14,10},{1,5},{3,7},... | collective-permute-start | bytes 1572872 | tf_op jit(solution)/shard_map/ppermute | solution.py:280
  51.0 41.3 %collective-permute-start.13 = (bf16[128,2048]{1,0:T(8,128)(2,1)}, bf16[128,2048]{1,0:T(8,128)(2,1)}, u32[]{:S(2)}, u32[]{:S(2)}) collective-permute-start(bf16[128,2048]{1,0:T(8,128)(2,1)} %refs_4_.1), channel_id=1, source_target_pairs={{4,8},{6,10},{8,4},{10,6},{5,9},{7,11},{9,5},{11,7},{20,24},{22,26... | collective-permute-start | bytes 1572872 | tf_op jit(solution)/shard_map/ppermute | solution.py:280
  54.6 37.8 %collective-permute-start.14 = (bf16[128,2048]{1,0:T(8,128)(2,1)}, bf16[128,2048]{1,0:T(8,128)(2,1)}, u32[]{:S(2)}, u32[]{:S(2)}) collective-permute-start(bf16[128,2048]{1,0:T(8,128)(2,1)} %refs_4_.1), channel_id=1, source_target_pairs={{0,2},{2,0},{4,6},{6,4},{8,10},{10,8},{12,14},{14,12},{1,3},{3,1},... | collective-permute-start | bytes 1572872 | tf_op jit(solution)/shard_map/ppermute | solution.py:280
  62.4 29.9 %collective-permute-start.11 = (bf16[128,2048]{1,0:T(8,128)(2,1)S(1)}, bf16[128,2048]{1,0:T(8,128)(2,1)}, u32[]{:S(2)}, u32[]{:S(2)}) collective-permute-start(bf16[128,2048]{1,0:T(8,128)(2,1)S(1)} %broadcast_select_fusion.8.refs_8_.refs_12_), channel_id=1, source_target_pairs={{0,2},{2,0},{4,6},{6,4},{8,10},{10,8},{12,14},{14,12},{1,3},{3,1},... | collective-permute-start | bytes 1572872 | tf_op jit(solution)/shard_map/ppermute | solution.py:280
  92.9 23.1 %collective-permute-start.19 = (bf16[896,2048]{1,0:T(8,128)(2,1)S(1)}, bf16[896,2048]{1,0:T(8,128)(2,1)S(1)}, u32[]{:S(2)}, u32[]{:S(2)}) collective-permute-start(bf16[896,2048]{1,0:T(8,128)(2,1)S(1)} %constant_dynamic-slice_fusion.1), channel_id=1, source_target_pairs={{0,1},{1,0},{2,3},{3,2},{4,5},{5,4},{6,7},{7,6},{8,9},{9,8},{10,11... | collective-permute-start | bytes 11010056 | tf_op jit(solution)/shard_map/ppermute | solution.py:285
  96.5 19.5 %collective-permute-start.20 = (bf16[896,2048]{1,0:T(8,128)(2,1)S(1)}, bf16[896,2048]{1,0:T(8,128)(2,1)S(1)}, u32[]{:S(2)}, u32[]{:S(2)}) collective-permute-start(bf16[896,2048]{1,0:T(8,128)(2,1)S(1)} %constant_dynamic-slice_fusion), channel_id=1, source_target_pairs={{0,1},{1,0},{2,3},{3,2},{4,5},{5,4},{6,7},{7,6},{8,9},{9,8},{10,11... | collective-permute-start | bytes 11010056 | tf_op jit(solution)/shard_map/ppermute | solution.py:285
  98.6 14.5 %collective-permute-start.17 = (bf16[128,2048]{1,0:T(8,128)(2,1)S(1)}, bf16[128,2048]{1,0:T(8,128)(2,1)}, u32[]{:S(2)}, u32[]{:S(2)}) collective-permute-start(bf16[128,2048]{1,0:T(8,128)(2,1)S(1)} %get-tuple-element.167), channel_id=1, source_target_pairs={{0,4},{2,6},{4,0},{6,2},{8,12},{10,14},{12,8},{14,10},{1,5},{3,7},... | collective-permute-start | bytes 1572872 | tf_op jit(solution)/shard_map/ppermute | solution.py:280
  101.1 12.8 %collective-permute-start.16 = (bf16[128,2048]{1,0:T(8,128)(2,1)S(1)}, bf16[128,2048]{1,0:T(8,128)(2,1)S(1)}, u32[]{:S(2)}, u32[]{:S(2)}) collective-permute-start(bf16[128,2048]{1,0:T(8,128)(2,1)S(1)} %copy-done.7), channel_id=1, source_target_pairs={{0,2},{2,0},{4,6},{6,4},{8,10},{10,8},{12,14},{14,12},{1,3},{3,1},... | collective-permute-start | bytes 1572872 | tf_op jit(solution)/shard_map/ppermute | solution.py:280
  101.3 14.6 %collective-permute-start.18 = (bf16[128,2048]{1,0:T(8,128)(2,1)}, bf16[128,2048]{1,0:T(8,128)(2,1)}, u32[]{:S(2)}, u32[]{:S(2)}) collective-permute-start(bf16[128,2048]{1,0:T(8,128)(2,1)} %collective-permute-done.12.refs_5_), channel_id=1, source_target_pairs={{4,8},{6,10},{8,4},{10,6},{5,9},{7,11},{9,5},{11,7},{20,24},{22,26... | collective-permute-start | bytes 1572872 | tf_op jit(solution)/shard_map/ppermute | solution.py:280
  119.7 22.5 %collective-permute-start.21 = (bf16[128,2048]{1,0:T(8,128)(2,1)}, bf16[128,2048]{1,0:T(8,128)(2,1)S(1)}, u32[]{:S(2)}, u32[]{:S(2)}) collective-permute-start(bf16[128,2048]{1,0:T(8,128)(2,1)} %get-tuple-element.168), channel_id=1, source_target_pairs={{0,2},{2,0},{4,6},{6,4},{8,10},{10,8},{12,14},{14,12},{1,3},{3,1},... | collective-permute-start | bytes 1572872 | tf_op jit(solution)/shard_map/ppermute | solution.py:280
  120.9 21.3 %collective-permute-start.22 = (bf16[128,2048]{1,0:T(8,128)(2,1)}, bf16[128,2048]{1,0:T(8,128)(2,1)}, u32[]{:S(2)}, u32[]{:S(2)}) collective-permute-start(bf16[128,2048]{1,0:T(8,128)(2,1)} %collective-permute-done.18), channel_id=1, source_target_pairs={{4,0},{6,2},{8,12},{10,14},{5,1},{7,3},{9,13},{11,15},{20,16},{22,... | collective-permute-start | bytes 1572872 | tf_op jit(solution)/shard_map/ppermute | solution.py:280
  123.0 19.2 %collective-permute-start.23 = (bf16[128,2048]{1,0:T(8,128)(2,1)}, bf16[128,2048]{1,0:T(8,128)(2,1)}, u32[]{:S(2)}, u32[]{:S(2)}) collective-permute-start(bf16[128,2048]{1,0:T(8,128)(2,1)} %collective-permute-done.17), channel_id=1, source_target_pairs={{4,8},{6,10},{8,4},{10,6},{5,9},{7,11},{9,5},{11,7},{20,24},{22,26... | collective-permute-start | bytes 1572872 | tf_op jit(solution)/shard_map/ppermute | solution.py:280
  145.5 19.6 %collective-permute-start.28 = (bf16[512,2048]{1,0:T(8,128)(2,1)S(1)}, bf16[512,2048]{1,0:T(8,128)(2,1)S(1)}, u32[]{:S(2)}, u32[]{:S(2)}) collective-permute-start(bf16[512,2048]{1,0:T(8,128)(2,1)S(1)} %pad_maximum_fusion.2), channel_id=1, source_target_pairs={{0,1},{1,0},{2,3},{3,2},{4,5},{5,4},{6,7},{7,6},{8,9},{9,8},{10,11... | collective-permute-start | bytes 6291464 | tf_op jit(solution)/shard_map/ppermute | solution.py:285
  146.2 18.8 %collective-permute-start.27 = (bf16[896,512]{1,0:T(8,128)(2,1)}, bf16[896,512]{1,0:T(8,128)(2,1)S(1)}, u32[]{:S(2)}, u32[]{:S(2)}) collective-permute-start(bf16[896,512]{1,0:T(8,128)(2,1)} %get-tuple-element.121.refs_0_), channel_id=1, source_target_pairs={{0,1},{1,0},{2,3},{3,2},{4,5},{5,4},{6,7},{7,6},{8,9},{9,8},{10,11... | collective-permute-start | bytes 2752520 | tf_op jit(solution)/shard_map/ppermute | solution.py:285
  146.3 18.8 %collective-permute-start.25 = (bf16[128,2048]{1,0:T(8,128)(2,1)}, bf16[128,2048]{1,0:T(8,128)(2,1)S(1)}, u32[]{:S(2)}, u32[]{:S(2)}) collective-permute-start(bf16[128,2048]{1,0:T(8,128)(2,1)} %collective-permute-done.17), channel_id=1, source_target_pairs={{0,2},{2,0},{12,14},{14,12},{1,3},{3,1},{13,15},{15,13},{16,18},{1... | collective-permute-start | bytes 1572872 | tf_op jit(solution)/shard_map/ppermute | solution.py:280
  147.0 18.1 %collective-permute-start.26 = (bf16[128,2048]{1,0:T(8,128)(2,1)}, bf16[128,2048]{1,0:T(8,128)(2,1)S(1)}, u32[]{:S(2)}, u32[]{:S(2)}) collective-permute-start(bf16[128,2048]{1,0:T(8,128)(2,1)} %collective-permute-done.23), channel_id=1, source_target_pairs={{4,0},{6,2},{8,12},{10,14},{5,1},{7,3},{9,13},{11,15},{20,16},{22,... | collective-permute-start | bytes 1572872 | tf_op jit(solution)/shard_map/ppermute | solution.py:280
  169.0 17.3 %collective-permute-start.29 = (bf16[512,2048]{1,0:T(8,128)(2,1)}, bf16[512,2048]{1,0:T(8,128)(2,1)S(1)}, u32[]{:S(2)}, u32[]{:S(2)}) collective-permute-start(bf16[512,2048]{1,0:T(8,128)(2,1)} %pad_maximum_fusion.3), channel_id=1, source_target_pairs={{0,1},{1,0},{2,3},{3,2},{4,5},{5,4},{6,7},{7,6},{8,9},{9,8},{10,11... | collective-permute-start | bytes 6291464 | tf_op jit(solution)/shard_map/ppermute | solution.py:285
  169.4 16.9 %collective-permute-start.30 = (bf16[896,512]{1,0:T(8,128)(2,1)S(1)}, bf16[896,512]{1,0:T(8,128)(2,1)S(1)}, u32[]{:S(2)}, u32[]{:S(2)}) collective-permute-start(bf16[896,512]{1,0:T(8,128)(2,1)S(1)} %copy-done.16), channel_id=1, source_target_pairs={{0,1},{1,0},{2,3},{3,2},{4,5},{5,4},{6,7},{7,6},{8,9},{9,8},{10,11... | collective-permute-start | bytes 2752520 | tf_op jit(solution)/shard_map/ppermute | solution.py:285
  186.3 17.7 %collective-permute-start.31 = (bf16[896,512]{1,0:T(8,128)(2,1)}, bf16[896,512]{1,0:T(8,128)(2,1)S(1)}, u32[]{:S(2)}, u32[]{:S(2)}) collective-permute-start(bf16[896,512]{1,0:T(8,128)(2,1)} %get-tuple-element.145.refs_0_), channel_id=1, source_target_pairs={{0,1},{1,0},{2,3},{3,2},{4,5},{5,4},{6,7},{7,6},{8,9},{9,8},{10,11... | collective-permute-start | bytes 2752520 | tf_op jit(solution)/shard_map/ppermute | solution.py:285
  186.8 17.3 %collective-permute-start.32 = (bf16[896,512]{1,0:T(8,128)(2,1)}, bf16[896,512]{1,0:T(8,128)(2,1)S(1)}, u32[]{:S(2)}, u32[]{:S(2)}) collective-permute-start(bf16[896,512]{1,0:T(8,128)(2,1)} %get-tuple-element.153.refs_2_), channel_id=1, source_target_pairs={{0,1},{1,0},{2,3},{3,2},{4,5},{5,4},{6,7},{7,6},{8,9},{9,8},{10,11... | collective-permute-start | bytes 2752520 | tf_op jit(solution)/shard_map/ppermute | solution.py:285
  204.1 13.5 %collective-permute-start.33 = (bf16[896,512]{1,0:T(8,128)(2,1)}, bf16[896,512]{1,0:T(8,128)(2,1)S(1)}, u32[]{:S(2)}, u32[]{:S(2)}) collective-permute-start(bf16[896,512]{1,0:T(8,128)(2,1)} %get-tuple-element.154.refs_1_), channel_id=1, source_target_pairs={{0,1},{1,0},{2,3},{3,2},{4,5},{5,4},{6,7},{7,6},{8,9},{9,8},{10,11... | collective-permute-start | bytes 2752520 | tf_op jit(solution)/shard_map/ppermute | solution.py:285
  204.6 13.0 %collective-permute-start.34 = (bf16[896,512]{1,0:T(8,128)(2,1)}, bf16[896,512]{1,0:T(8,128)(2,1)S(1)}, u32[]{:S(2)}, u32[]{:S(2)}) collective-permute-start(bf16[896,512]{1,0:T(8,128)(2,1)} %get-tuple-element.155.refs_3_), channel_id=1, source_target_pairs={{0,1},{1,0},{2,3},{3,2},{4,5},{5,4},{6,7},{7,6},{8,9},{9,8},{10,11... | collective-permute-start | bytes 2752520 | tf_op jit(solution)/shard_map/ppermute | solution.py:285
  (32 other events, 491.6 us)
